TPU v7x, 32 devices: a whole 2x2x4 slice. The times are simulated.
32 devices in a mesh: groups: 2 (over x), lat: 16 (over z, y, core).
Axes of the slice: x: 2, y: 2, z: 4, core: 2. Of those that a mesh axis runs over, the one named last changes fastest.
Arguments:
- objects: float32 [2, 2, 8192, 1024], P(None, None, ('groups', 'lat')), parts along dimension 2, may hold values from -5 to 5
- probes: float32 [4, 2, 256, 256], P('groups'), parts along dimension 0, may hold values from -5 to 5
- x_offsets: int32 [64], P(('groups', 'lat')), parts along dimension 0, may hold values from 0 to 255
- y_offsets: int32 [64], P(('groups', 'lat')), parts along dimension 0, may hold values from 0 to 768
- modes: int32 [64], P(('groups', 'lat')), parts along dimension 0, may hold values from 0 to 1
- measured: float32 [64, 256, 256], P(('groups', 'lat')), parts along dimension 0, may hold values from 0 to 2
Outputs:
- updated: float32 [2, 2, 8192, 1024], P(None, None, ('groups', 'lat')), parts along dimension 2
There are 2 independent parts, one for each index of `groups`. A program takes and returns all parts, laid end to end along the dimension named above; each array names one. Nothing has to cross between parts.
All inputs are finite; a program needn't handle non-finite values.
Results may differ from a plain program's by a relative error of at most 0.0003.
Values sent between devices are 32-bit elements; how exact they have to be, the bound alone decides.
A program may use at most 128 MiB of HBM per device.

v0:
```python
import math

import jax
import jax.numpy as jnp
from jax import lax
from jax.sharding import PartitionSpec as P

W = 256
TILE = 256
SLICES = 2
NPROBE = 2


spread_phase = 40.0
descent_rate = 1.0
highest = lax.Precision.HIGHEST


def from_behind(block, axis, distance):
    devices = range(lax.axis_size(axis))
    route = [(i - distance, i) for i in devices if i - distance in devices]
    return lax.ppermute(block, axis, route)


def kernel_phase(width):
    counter = jnp.arange(width, dtype=jnp.int32)
    folded = ((counter + width // 2) % width - width // 2).astype(jnp.float32) / width
    return spread_phase * (folded[:, None] ** 2 + folded[None, :] ** 2)


def fourier_tables(width):
    counter = jnp.arange(width, dtype=jnp.int32)
    wound = counter[:, None] * counter[None, :] % width
    angles = wound.astype(jnp.float32) * (2.0 * math.pi / width)
    scaling = 1.0 / math.sqrt(width)
    return (jnp.cos(angles) * scaling, jnp.sin(angles) * scaling)


def fourier_pair(real_part, imag_part, tables, direction):
    cosines, sines = tables
    signed = direction * sines
    last_real = jnp.einsum("pjk,kl->pjl", real_part, cosines, precision=highest) - jnp.einsum(
        "pjk,kl->pjl", imag_part, signed, precision=highest
    )
    last_imag = jnp.einsum("pjk,kl->pjl", imag_part, cosines, precision=highest) + jnp.einsum(
        "pjk,kl->pjl", real_part, signed, precision=highest
    )
    first_real = jnp.einsum("kj,pjl->pkl", cosines, last_real, precision=highest) - jnp.einsum(
        "kj,pjl->pkl", signed, last_imag, precision=highest
    )
    first_imag = jnp.einsum("kj,pjl->pkl", cosines, last_imag, precision=highest) + jnp.einsum(
        "kj,pjl->pkl", signed, last_real, precision=highest
    )
    return (first_real, first_imag)


def propagate(real_part, imag_part, tables, kernel_real, kernel_imag):
    spec_real, spec_imag = fourier_pair(real_part, imag_part, tables, -1.0)
    moved_real = spec_real * kernel_real - spec_imag * kernel_imag
    moved_imag = spec_real * kernel_imag + spec_imag * kernel_real
    return fourier_pair(moved_real, moved_imag, tables, 1.0)


def gradient_windows(windows, chosen, measured, tables, kernel_real, kernel_imag):
    wave_real, wave_imag = (chosen[:, 0], chosen[:, 1])
    entering = []
    for s in range(SLICES):
        if s > 0:
            wave_real, wave_imag = propagate(wave_real, wave_imag, tables, kernel_real, kernel_imag)
        entering.append((wave_real, wave_imag))
        slab_real, slab_imag = (windows[:, s, 0], windows[:, s, 1])
        wave_real, wave_imag = (
            wave_real * slab_real - wave_imag * slab_imag,
            wave_real * slab_imag + wave_imag * slab_real,
        )
    far_real, far_imag = fourier_pair(wave_real, wave_imag, tables, -1.0)
    residual = far_real * far_real + far_imag * far_imag - measured
    back_real, back_imag = fourier_pair(residual * far_real, residual * far_imag, tables, 1.0)
    pieces = [None] * SLICES
    for s in reversed(range(SLICES)):
        in_real, in_imag = entering[s]
        pieces[s] = jnp.stack(
            [in_real * back_real + in_imag * back_imag, in_real * back_imag - in_imag * back_real],
            axis=1,
        )
        slab_real, slab_imag = (windows[:, s, 0], windows[:, s, 1])
        back_real, back_imag = (
            slab_real * back_real + slab_imag * back_imag,
            slab_real * back_imag - slab_imag * back_real,
        )
        if s > 0:
            back_real, back_imag = propagate(
                back_real, back_imag, tables, kernel_real, -kernel_imag
            )
    return jnp.stack(pieces, axis=1)


def on_device(objects, probes, x_offsets, y_offsets, modes, measured):
    anchor = jnp.zeros((), jnp.int32)
    amount = x_offsets.shape[0]
    tables = fourier_tables(W)
    phase_map = kernel_phase(W)
    kernel_real = jnp.cos(phase_map)
    kernel_imag = -jnp.sin(phase_map)
    selector = modes[:, None] == jnp.arange(NPROBE, dtype=jnp.int32)[None, :]
    chosen = jnp.sum(jnp.where(selector[:, :, None, None, None], probes[None], 0.0), axis=1)
    neighbour = from_behind(objects, "lat", -1)
    extended = jnp.concatenate([objects, neighbour], axis=2)

    def fetch(x_offset, y_offset):
        return lax.dynamic_slice(extended, (anchor, anchor, x_offset, y_offset), (SLICES, 2, W, W))

    windows = jax.vmap(fetch)(x_offsets, y_offsets)
    pieces = gradient_windows(windows, chosen, measured, tables, kernel_real, kernel_imag)

    def add_window(i, buffer):
        corner = (anchor, anchor, x_offsets[i], y_offsets[i])
        current = lax.dynamic_slice(buffer, corner, (SLICES, 2, W, W))
        return lax.dynamic_update_slice(buffer, current + pieces[i], corner)

    buffer = lax.fori_loop(0, amount, add_window, jnp.zeros_like(extended))
    returned = from_behind(buffer[:, :, TILE:], "lat", 1)
    gradient = buffer[:, :, :TILE] + returned
    return objects - descent_rate * gradient


def solution(mesh):
    in_specs = (
        P(None, None, ("groups", "lat"), None),
        P("groups", None, None, None),
        P(("groups", "lat")),
        P(("groups", "lat")),
        P(("groups", "lat")),
        P(("groups", "lat"), None, None),
    )
    out_specs = P(None, None, ("groups", "lat"), None)
    return jax.shard_map(
        on_device, mesh=mesh, in_specs=in_specs, out_specs=out_specs, check_vma=False
    )
```

profile of v0, /device:TPU:8, one launch (start us, length us, event | category | flops | bytes accessed | tf_op | source)
XLA Modules:
  0.0 266.9 jit_solution(11585928870141830070)
XLA Ops:
  0.0 2.7 %collective-permute-start = (f32[2,2,256,1024]{3,2,1,0:T(8,128)}, f32[2,2,256,1024]{3,2,1,0:T(8,128)}, u32[]{:S(2)}, u32[]{:S(2)}) collective-permute-start(f32[2,2,256,1024]{3,2,1,0:T(8,128)} %param.8), channel_id=1, source_target_pairs={{1,0},{2,1},{3,2},{4,3},{5,4},{6,5},{7,6},{8,7},{9,8},{10,9},{11,1... | collective-permute-start | bytes 12582920 | tf_op jit(solution)/shard_map/ppermute | solution.py:22
  11.1 38.0 %collective-permute-done = f32[2,2,256,1024]{3,2,1,0:T(8,128)} collective-permute-done((f32[2,2,256,1024]{3,2,1,0:T(8,128)}, f32[2,2,256,1024]{3,2,1,0:T(8,128)}, u32[]{:S(2)}, u32[]{:S(2)}) %collective-permute-start) | collective-permute-done | bytes 4194336 | tf_op jit(solution)/shard_map/ppermute | solution.py:22
  49.1 8.3 %pad_maximum_fusion = f32[2,2,512,1024]{3,2,1,0:T(8,128)} fusion(f32[2,2,256,1024]{3,2,1,0:T(8,128)} %collective-permute-done, f32[2,2,256,1024]{3,2,1,0:T(8,128)} %param.8), kind=kLoop, calls=%fused_computation.5 | loop fusion | flops 2097152 | bytes 16777216 | tf_op jit(solution)/shard_map/concatenate | solution.py:108
  57.4 10.4 %while.15 = (s32[]{:T(128)}, f32[2,2,512,1024]{3,2,1,0:T(8,128)}, s32[2,4]{1,0:T(2,128)S(1)}, f32[2,2,2,256,256]{3,4,0,2,1:T(8,128)}, s32[]{:T(128)}) while((s32[]{:T(128)}, f32[2,2,512,1024]{3,2,1,0:T(8,128)}, s32[2,4]{1,0:T(2,128)S(1)}, f32[2,2,2,256,256]{3,4,0,2,1:T(8,128)}, s32[]{:T(128)}) %tuple.56), condition=%wide.while_cond, body=%wide.while_body.sunk | while | flops 2 | bytes 6291589 | solution.py:111
  58.0 3.0 %dynamic-slice_bitcast_fusion.2 = f32[1,2,2,256,256]{4,3,2,1,0:T(8,128)S(1)} fusion(f32[2,2,512,1024]{3,2,1,0:T(8,128)} %get-tuple-element.229, s32[]{:T(128)} %bitcast.265, s32[]{:T(128)} %bitcast.266), kind=kLoop, calls=%fused_computation.2.clone.1 | loop fusion | bytes 2097160 | tf_op jit(solution)/shard_map/vmap()/gather
  63.0 3.0 %dynamic-slice_bitcast_fusion.2 = f32[1,2,2,256,256]{4,3,2,1,0:T(8,128)S(1)} fusion(f32[2,2,512,1024]{3,2,1,0:T(8,128)} %get-tuple-element.229, s32[]{:T(128)} %bitcast.265, s32[]{:T(128)} %bitcast.266), kind=kLoop, calls=%fused_computation.2.clone.1 | loop fusion | bytes 2097160 | tf_op jit(solution)/shard_map/vmap()/gather
  69.5 1.8 fusion.97
  71.3 1.8 fusion.93
  73.1 1.8 convolution_subtract_fusion.11
  75.0 1.8 convolution_add_fusion.11
  76.8 1.8 fusion.91
  78.7 1.8 fusion.95
  80.5 2.0 fusion.10
  82.5 1.8 fusion.11
  84.4 1.9 fusion.85
  86.2 1.9 fusion.89
  88.1 1.9 convolution_add_fusion.9
  90.0 1.8 fusion.83
  91.8 2.1 convolution_subtract_fusion.9
  93.9 1.8 fusion.87
  95.8 1.8 fusion.8
  97.6 1.9 fusion.13
  99.5 1.8 fusion.77
  101.3 1.8 fusion.81
  103.2 2.2 convolution_add_fusion.7
  105.4 1.8 convolution_subtract_fusion.7
  107.2 1.8 fusion.79
  109.1 1.8 fusion.75
  110.9 1.8 fusion.7
  112.7 1.8 fusion.6
  114.6 1.9 fusion.69
  116.5 2.1 fusion.73
  118.6 1.9 convolution_add_fusion.5
  120.5 1.8 fusion.67
  122.3 1.9 convolution_subtract_fusion.5
  124.3 1.8 fusion.71
  126.1 1.8 fusion.4
  128.0 2.2 fusion.14
  130.2 1.8 fusion.65
  132.0 1.8 fusion.61
  133.9 1.9 convolution_subtract_fusion.3
  135.8 1.9 convolution_add_fusion.3
  137.6 1.8 fusion.59
  139.5 2.3 fusion.63
  141.8 1.8 fusion.2
  143.6 1.8 fusion.3
  145.5 1.9 fusion.53
  147.3 1.9 fusion.57
  149.2 1.9 convolution_add_fusion.1
  151.1 1.8 fusion.51
  153.0 2.1 convolution_subtract_fusion.1
  155.0 1.8 fusion.55
  156.8 1.8 fusion
  158.7 1.9 fusion.19
  162.2 4.3 %broadcast_in_dim.26 = f32[2,2,512,1024]{3,2,1,0:T(8,128)} broadcast(f32[]{:T(128)} %constant.73.clone.1), dimensions={} | broadcast | bytes 8388612 | tf_op jit(solution)/shard_map/broadcast_in_dim | solution.py:121
  166.5 40.8 %while.14 = (s32[]{:T(128)}, f32[2,2,512,1024]{3,2,1,0:T(8,128)}, s32[2]{0:T(128)S(1)}, s32[2]{0:T(128)S(1)}, f32[2,2,2,256,256]{3,4,0,2,1:T(8,128)}, /*index=5*/s32[]{:T(128)}, s32[]{:T(128)}, s32[]{:T(128)}, s32[]{:T(128)}) while((s32[]{:T(128)}, f32[2,2,512,1024]{3,2,1,0:T(8,128)}, s32[2]{0:T(128)S(1)}, s32[2]{0:T(128)S(1)}, ...), condition=%wide.region_2.3_spmd, body=%wide.region_1.2_spmd.sunk | while | flops 262152 | bytes 9437393 | solution.py:121
  173.1 1.8 bitcast_add_fusion.2
  174.9 11.7 %dynamic_update_slice.8 = f32[2,2,512,1024]{3,2,1,0:T(8,128)} dynamic-update-slice(f32[2,2,512,1024]{3,2,1,0:T(8,128)} %get-tuple-element.243, f32[2,2,256,256]{3,2,1,0:T(8,128)S(1)} %bitcast_add_fusion.2, s32[]{:T(128)} %constant.72.clone.1..sunk, s32[]{:T(128)} %constant.72.clone.1..sunk, s32[]{:T(128)S(6)} %select_n.348, s32[]{:T(128)S(6)} %select_n.349) | dynamic-update-slice | bytes 2097156 | tf_op jit(solution)/shard_map/while/body/eval_jaxpr/dynamic_update_slice | solution.py:119
  193.2 1.8 bitcast_add_fusion.2
  195.0 12.3 %dynamic_update_slice.8 = f32[2,2,512,1024]{3,2,1,0:T(8,128)} dynamic-update-slice(f32[2,2,512,1024]{3,2,1,0:T(8,128)} %get-tuple-element.243, f32[2,2,256,256]{3,2,1,0:T(8,128)S(1)} %bitcast_add_fusion.2, s32[]{:T(128)} %constant.72.clone.1..sunk, s32[]{:T(128)} %constant.72.clone.1..sunk, s32[]{:T(128)S(6)} %select_n.348, s32[]{:T(128)S(6)} %select_n.349) | dynamic-update-slice | bytes 2097156 | tf_op jit(solution)/shard_map/while/body/eval_jaxpr/dynamic_update_slice | solution.py:119
  207.3 2.7 slice.33
  209.9 3.4 %collective-permute-start.1 = (f32[2,2,256,1024]{3,2,1,0:T(8,128)S(1)}, f32[2,2,256,1024]{3,2,1,0:T(8,128)S(1)}, u32[]{:S(2)}, u32[]{:S(2)}) collective-permute-start(f32[2,2,256,1024]{3,2,1,0:T(8,128)S(1)} %slice.33), channel_id=1, source_target_pairs={{0,1},{1,2},{2,3},{3,4},{4,5},{5,6},{6,7},{7,8},{8,9},{9,10},{10,1... | collective-permute-start | bytes 12582920 | tf_op jit(solution)/shard_map/ppermute | solution.py:22
  213.3 47.7 %collective-permute-done.1 = f32[2,2,256,1024]{3,2,1,0:T(8,128)S(1)} collective-permute-done((f32[2,2,256,1024]{3,2,1,0:T(8,128)S(1)}, f32[2,2,256,1024]{3,2,1,0:T(8,128)S(1)}, u32[]{:S(2)}, u32[]{:S(2)}) %collective-permute-start.1) | collective-permute-done | bytes 4194336 | tf_op jit(solution)/shard_map/ppermute | solution.py:22
  261.0 5.7 %add_subtract_fusion = f32[2,2,256,1024]{3,2,1,0:T(8,128)} fusion(f32[2,2,256,1024]{3,2,1,0:T(8,128)} %param.8, f32[2,2,256,1024]{3,2,1,0:T(8,128)S(1)} %collective-permute-done.1, f32[2,2,512,1024]{3,2,1,0:T(8,128)S(1)} %copy-done), kind=kLoop, calls=%fused_computation.6 | loop fusion | flops 2097152 | bytes 16777216 | tf_op jit(solution)/shard_map/sub | solution.py:124
  (47 shorter events, 21.3 us)
Async XLA Ops:
  0.0 49.1 %collective-permute-start = (f32[2,2,256,1024]{3,2,1,0:T(8,128)}, f32[2,2,256,1024]{3,2,1,0:T(8,128)}, u32[]{:S(2)}, u32[]{:S(2)}) collective-permute-start(f32[2,2,256,1024]{3,2,1,0:T(8,128)} %param.8), channel_id=1, source_target_pairs={{1,0},{2,1},{3,2},{4,3},{5,4},{6,5},{7,6},{8,7},{9,8},{10,9},{11,1... | collective-permute-start | bytes 12582920 | tf_op jit(solution)/shard_map/ppermute | solution.py:22
  88.1 9.5 %copy-start.3 = (f32[2,2,2,256,256]{3,4,0,2,1:T(8,128)S(1)}, f32[2,2,2,256,256]{3,4,0,2,1:T(8,128)}, u32[]{:S(2)}) copy-start(f32[2,2,2,256,256]{3,4,0,2,1:T(8,128)} %get-tuple-element.107) | copy-start | bytes 6291460
  149.2 9.4 %copy-start.1 = (f32[2,1,256,256]{2,3,0,1:T(8,128)S(1)}, f32[2,1,256,256]{2,3,0,1:T(8,128)}, u32[]{:S(2)}) copy-start(f32[2,1,256,256]{2,3,0,1:T(8,128)} %copy.172) | copy-start | bytes 1572868
  149.2 9.4 %copy-start.2 = (f32[2,1,256,256]{2,3,0,1:T(8,128)S(1)}, f32[2,1,256,256]{2,3,0,1:T(8,128)}, u32[]{:S(2)}) copy-start(f32[2,1,256,256]{2,3,0,1:T(8,128)} %copy.173) | copy-start | bytes 1572868
  162.2 4.3 %copy-start.4 = (s32[2]{0:T(128)S(1)}, s32[2]{0:T(128)}, u32[]{:S(2)}) copy-start(s32[2]{0:T(128)} %param.10) | copy-start | bytes 28
  162.2 4.3 %copy-start.5 = (s32[2]{0:T(128)S(1)}, s32[2]{0:T(128)}, u32[]{:S(2)}) copy-start(s32[2]{0:T(128)} %param.11) | copy-start | bytes 28
  207.3 53.7 %copy-start = (f32[2,2,512,1024]{3,2,1,0:T(8,128)S(1)}, f32[2,2,512,1024]{3,2,1,0:T(8,128)}, u32[]{:S(2)}) copy-start(f32[2,2,512,1024]{3,2,1,0:T(8,128)} %get-tuple-element.99) | copy-start | bytes 25165828
  209.9 51.1 %collective-permute-start.1 = (f32[2,2,256,1024]{3,2,1,0:T(8,128)S(1)}, f32[2,2,256,1024]{3,2,1,0:T(8,128)S(1)}, u32[]{:S(2)}, u32[]{:S(2)}) collective-permute-start(f32[2,2,256,1024]{3,2,1,0:T(8,128)S(1)} %slice.33), channel_id=1, source_target_pairs={{0,1},{1,2},{2,3},{3,4},{4,5},{5,6},{6,7},{7,8},{8,9},{9,10},{10,1... | collective-permute-start | bytes 12582920 | tf_op jit(solution)/shard_map/ppermute | solution.py:22
where the time goes:
time: 272 us; the launch traced here: 267 us
  matrix products  90.6 us (33%)
  waiting for transfers between devices  85.7 us (32%)
  local copies, waits for them, and re-layouts  50.1 us (18%)
  other arithmetic  25.8 us (9%)
  loops' own time  7.97 us (3%)
  starting transfers between devices  6.13 us (2%)
    ppermute x2, waiting for transfers between devices, from_behind(): return lax.ppermute(block, axis, route)  85.7 us
    dynamic_update_slice x2, local copies, waits for them, and re-layouts, add_window(): return lax.dynamic_update_slice(buffer, current + pieces[i], corner)  24 us
    dot_general x6, matrix products, fourier_pair(): jnp.einsum('pjk,kl->pjl', real_part, signed, precision=highest)  11.6 us
    dot_general x6, matrix products, fourier_pair(): jnp.einsum('pjk,kl->pjl', imag_part, signed, precision=highest)  11.6 us
    dot_general x6, matrix products, fourier_pair(): jnp.einsum('kj,pjl->pkl', signed, last_imag, precision=highest)  11.5 us
    dot_general x6, matrix products, fourier_pair(): jnp.einsum('kj,pjl->pkl', cosines, last_real, precision=highest)  11.4 us
    dot_general x6, matrix products, fourier_pair(): jnp.einsum('pjk,kl->pjl', real_part, cosines, precision=highest)  11.3 us
    dot_general x6, matrix products, fourier_pair(): jnp.einsum('pjk,kl->pjl', imag_part, cosines, precision=highest)  11.1 us
  transfers between devices with their start and end apart: 2, of which 2 were waited for; matrix products, arithmetic and copies ran while one was open for 3% of the time, Pallas kernels for 0%

commit v1 on v0

v1 whole, which is shorter than its diff:
```python
import functools

import jax
import jax.numpy as jnp
import ml_dtypes
import numpy as np
from jax import lax
from jax.experimental import pallas as pl
from jax.experimental.pallas import tpu as pltpu
from jax.sharding import PartitionSpec as P

spread_phase = 40.0
descent_rate = 1.0
VMEM_BYTES = 48 * 1024 * 1024


def from_behind(block, axis, distance):
    devices = range(lax.axis_size(axis))
    route = [(i - distance, i) for i in devices if i - distance in devices]
    return lax.ppermute(block, axis, route)


def split_table(table):
    high = table.astype(ml_dtypes.bfloat16)
    low = (table - high.astype(np.float64)).astype(ml_dtypes.bfloat16)
    return high, low


def tables(width):
    counter = np.arange(width)
    fourier = np.exp(-2j * np.pi * (np.outer(counter, counter) % width) / width) / np.sqrt(width)
    folded = ((counter + width // 2) % width - width // 2) / width
    phase = np.exp(-1j * spread_phase * folded**2)
    moving = np.conj(fourier) @ (phase[:, None] * fourier)
    rights, lefts = [], []
    for matrix in (moving, fourier):
        real, imag = matrix.real, matrix.imag
        high, low = split_table(np.block([[real, imag], [-imag, real]]))
        rights.append(np.concatenate([high, high, low], axis=0))
        high, low = split_table(np.block([[real, -imag], [imag, real]]))
        lefts.append(np.concatenate([high, high, low], axis=1))
    return np.stack(rights), np.stack(lefts)


def halves(values):
    high = values.astype(jnp.bfloat16)
    low = (values - high.astype(jnp.float32)).astype(jnp.bfloat16)
    return high, low


def transform(real, imag, right, left):
    width = real.shape[0]
    high, low = halves(jnp.concatenate([real, imag], axis=1))
    rows = jnp.dot(
        jnp.concatenate([high, low, high], axis=1), right, preferred_element_type=jnp.float32
    )
    high, low = halves(jnp.concatenate([rows[:, :width], rows[:, width:]], axis=0))
    both = jnp.dot(
        left, jnp.concatenate([high, low, high], axis=0), preferred_element_type=jnp.float32
    )
    return both[:width], both[width:]


def times(a, b):
    return a[0] * b[0] - a[1] * b[1], a[0] * b[1] + a[1] * b[0]


def pack_kernel(place, first, second, out):
    width = first.shape[-1]
    column = lax.broadcasted_iota(jnp.int32, (width, width), 1)
    turned = column < place[1] % width
    for s in range(first.shape[0]):
        for c in range(2):
            out[s, c] = jnp.where(turned, second[s, c], first[s, c])


def position_kernel(place, first, second, beyond, probe, measured, right, left, out):
    width = first.shape[-1]
    x, shift = place[0], place[1] % width
    row = lax.broadcasted_iota(jnp.int32, (width, width), 0)
    column = lax.broadcasted_iota(jnp.int32, (width, width), 1)
    inside, turned = row >= x, column < shift

    def window(s, c):
        own = jnp.where(turned, second[s, c], first[s, c])
        return jnp.where(inside, own, beyond[s, c])

    def rolled(c):
        return pltpu.roll(pltpu.roll(probe[0, c], x, 0), shift, 1)

    move, far = (right[0], left[0]), (right[1], left[1])
    entry = (rolled(0), rolled(1))
    slab = (window(1, 0), window(1, 1))
    middle = transform(*times(entry, (window(0, 0), window(0, 1))), *move)
    psi = transform(*times(middle, slab), *far)
    residual = psi[0] * psi[0] + psi[1] * psi[1] - measured[0]
    back = transform(residual * psi[0], -(residual * psi[1]), *far)
    piece = times(middle, back)
    out[1, 0] = piece[0]
    out[1, 1] = -piece[1]
    back = transform(*times(slab, back), *move)
    piece = times(entry, back)
    out[0, 0] = piece[0]
    out[0, 1] = -piece[1]


def update_kernel(places, objects, piece0, piece1, back0, back1, out):
    width = objects.shape[-1]
    block = pl.program_id(0)
    row = lax.broadcasted_iota(jnp.int32, (width, width), 0)
    column = lax.broadcasted_iota(jnp.int32, (width, width), 1) + block * width
    masks = []
    for k in range(4):
        x, y = places[k, 0], places[k, 1]
        across = (column >= y) & (column < y + width)
        masks.append(across & ((row >= x) if k < 2 else (row < x)))
    for s in range(objects.shape[0]):
        for c in range(2):
            total = objects[s, c]
            for mask, piece in zip(masks, (piece0, piece1, back0, back1)):
                total = total - descent_rate * jnp.where(mask, piece[s, c], 0.0)
            out[s, c] = total


def on_device(objects, probes, x_offsets, y_offsets, modes, measured):
    slices, _, tile, span = objects.shape
    width = measured.shape[1]
    blocks = span // width
    amount = x_offsets.shape[0]
    right, left = tables(width)
    right, left = jnp.asarray(right), jnp.asarray(left)
    window = (slices, 2, width, width)
    params = pltpu.CompilerParams(vmem_limit_bytes=VMEM_BYTES)

    own = jnp.stack([x_offsets, y_offsets, modes], axis=1)
    previous = from_behind(own, "lat", 1)

    lower = pl.BlockSpec(window, lambda i, place: (0, 0, 0, place[1] // width))
    upper = pl.BlockSpec(
        window, lambda i, place: (0, 0, 0, jnp.minimum(place[1] // width + 1, blocks - 1))
    )
    whole = pl.BlockSpec(window, lambda i, place: (0, 0, 0, 0))

    def pack(place):
        return pl.pallas_call(
            pack_kernel,
            grid_spec=pltpu.PrefetchScalarGridSpec(
                num_scalar_prefetch=1, grid=(1,), in_specs=[lower, upper], out_specs=whole
            ),
            out_shape=jax.ShapeDtypeStruct(window, jnp.float32),
            compiler_params=params,
            cost_estimate=pl.CostEstimate(flops=0, bytes_accessed=3 << 20, transcendentals=0),
            name="pack",
        )(place, objects, objects)

    def position(place, beyond, k):
        return pl.pallas_call(
            position_kernel,
            grid_spec=pltpu.PrefetchScalarGridSpec(
                num_scalar_prefetch=1,
                grid=(1,),
                in_specs=[
                    lower,
                    upper,
                    whole,
                    pl.BlockSpec((1, 2, width, width), lambda i, place: (place[2], 0, 0, 0)),
                    pl.BlockSpec((1, width, width), lambda i, place: (k, 0, 0)),
                    pl.BlockSpec(right.shape, lambda i, place: (0, 0, 0)),
                    pl.BlockSpec(left.shape, lambda i, place: (0, 0, 0)),
                ],
                out_specs=whole,
            ),
            out_shape=jax.ShapeDtypeStruct(window, jnp.float32),
            compiler_params=params,
            cost_estimate=pl.CostEstimate(
                flops=8 * 2 * 6 * 2 * width**3, bytes_accessed=10 << 20, transcendentals=0
            ),
            name="position",
        )(place, objects, objects, beyond, probes, measured, right, left)

    packed = [pack(previous[k]) for k in range(amount)]
    beyond = [from_behind(block, "lat", -1) for block in packed]
    pieces = [position(own[k], beyond[k], k) for k in range(amount)]
    returned = [from_behind(piece, "lat", 1) for piece in pieces]
    strip = pl.BlockSpec(window, lambda i, places: (0, 0, 0, i))
    fixed = pl.BlockSpec(window, lambda i, places: (0, 0, 0, 0))
    return pl.pallas_call(
        update_kernel,
        grid_spec=pltpu.PrefetchScalarGridSpec(
            num_scalar_prefetch=1,
            grid=(blocks,),
            in_specs=[strip] + [fixed] * 4,
            out_specs=strip,
        ),
        out_shape=jax.ShapeDtypeStruct(objects.shape, jnp.float32),
        compiler_params=params,
        name="update",
    )(jnp.concatenate([own, previous], axis=0), objects, *pieces, *returned)


def solution(mesh):
    in_specs = (
        P(None, None, ("groups", "lat"), None),
        P("groups", None, None, None),
        P(("groups", "lat")),
        P(("groups", "lat")),
        P(("groups", "lat")),
        P(("groups", "lat"), None, None),
    )
    out_specs = P(None, None, ("groups", "lat"), None)
    return jax.shard_map(
        on_device, mesh=mesh, in_specs=in_specs, out_specs=out_specs, check_vma=False
    )
```

time: 272 us -> 73.1 us (0.27); the launches traced: 267 us -> 72.6 us
  matrix products: 90.6 us -> 0 us
  waiting for transfers between devices: 85.7 us -> 27.9 us
  local copies, waits for them, and re-layouts: 50.1 us -> 4.43 us
  Pallas kernels: 0 us -> 28.8 us
  other arithmetic: 25.8 us -> 0.15 us
  loops' own time: 7.97 us -> 0 us
  starting transfers between devices: 6.13 us -> 11.2 us
    dot_general x48 -> x0, matrix products: 90.6 us -> none  [the longest x6 11.6 us: fourier_pair(): jnp.einsum('pjk,kl->pjl', real_part, signed, precision=highest)]
    ppermute x2 -> x5, waiting for transfers between devices: 85.7 us -> 27.9 us  [from_behind(): return lax.ppermute(block, axis, route)]
    pallas_call x0 -> x5, Pallas kernels: none -> 28.8 us  [the longest x2 21 us: position(): pl.pallas_call(position_kernel, grid_spec=pltpu.PrefetchScalarGridSpec(nu...]
    dynamic_update_slice x2 -> x0, local copies, waits for them, and re-layouts: 24 us -> none  [add_window(): return lax.dynamic_update_slice(buffer, current + pieces[i], corner)]
    gather x10 -> x0, local copies, waits for them, and re-layouts: 9.92 us -> none
    concatenate x2 -> x1, other arithmetic: 8.42 us -> 0.08 us  [on_device(): jnp.concatenate([own, previous], axis=0)]
    another operation x2 -> x0, loops' own time: 7.97 us -> none  [the longest x1 7.51 us: on_device(): buffer = lax.fori_loop(0, amount, add_window, jnp.zeros_like(extended))]
    sub x2 -> x0, other arithmetic: 7.4 us -> none  [the longest x1 5.73 us: on_device(): return objects - descent_rate * gradient]
  transfers between devices with their start and end apart: 2 -> 5, of which waited for: 2 -> 4; matrix products, arithmetic and copies ran while one was open for 3% -> 0% of each run, Pallas kernels for 0% -> 30%
where the time goes in v1:
time: 73.1 us; the launch traced here: 72.6 us
  Pallas kernels  28.8 us (39%)
  waiting for transfers between devices  27.9 us (38%)
  starting transfers between devices  11.2 us (15%)
  local copies, waits for them, and re-layouts  4.43 us (6%)
    ppermute x5, waiting for transfers between devices, from_behind(): return lax.ppermute(block, axis, route)  27.9 us
    pallas_call x2, Pallas kernels, position(): pl.pallas_call(position_kernel, grid_spec=pltpu.PrefetchScalarGridSpec(nu...  21 us
    ppermute x5, starting transfers between devices, from_behind(): return lax.ppermute(block, axis, route)  11.2 us
    pallas_call x1, Pallas kernels, on_device(): pl.pallas_call(update_kernel, grid_spec=pltpu.PrefetchScalarGridSpec(num_...  6.37 us
    another operation x3, local copies, waits for them, and re-layouts, on_device(): own = jnp.stack([x_offsets, y_offsets, modes], axis=1)  2.22 us
    unnamed x8, local copies, waits for them, and re-layouts  2.2 us
  transfers between devices with their start and end apart: 5, of which 4 were waited for; matrix products, arithmetic and copies ran while one was open for 0% of the time, Pallas kernels for 30%

profile of v1, /device:TPU:8, one launch (start us, length us, event | category | flops | bytes accessed | tf_op | source)
XLA Modules:
  0.0 72.6 jit_solution(3601451867166776408)
XLA Ops:
  0.0 0.7 %copy.9 = s32[2,1]{1,0:T(2,128)S(1)} copy(s32[2,1]{0,1:T(1,128)} %bitcast.11) | data formatting | bytes 16 | tf_op jit(solution)/shard_map/stack | solution.py:135
  0.7 0.7 %copy.10 = s32[2,1]{1,0:T(2,128)S(1)} copy(s32[2,1]{0,1:T(1,128)} %bitcast.12) | data formatting | bytes 16 | tf_op jit(solution)/shard_map/stack | solution.py:135
  1.5 0.7 %copy.11 = s32[2,1]{1,0:T(2,128)S(1)} copy(s32[2,1]{0,1:T(1,128)} %bitcast.13) | data formatting | bytes 16 | tf_op jit(solution)/shard_map/stack | solution.py:135
  2.2 0.1 pad_add_fusion.1
  2.3 1.9 %collective-permute-start = (s32[2,3]{1,0:T(2,128)S(1)}, s32[2,3]{1,0:T(2,128)S(1)}, u32[]{:S(2)}, u32[]{:S(2)}) collective-permute-start(s32[2,3]{1,0:T(2,128)S(1)} %pad_add_fusion.1), channel_id=1, source_target_pairs={{0,1},{1,2},{2,3},{3,4},{4,5},{5,6},{6,7},{7,8},{8,9},{9,10},{10,1... | collective-permute-start | bytes 80 | tf_op jit(solution)/shard_map/ppermute | solution.py:20
  4.2 3.9 %collective-permute-done = s32[2,3]{1,0:T(2,128)S(1)} collective-permute-done((s32[2,3]{1,0:T(2,128)S(1)}, s32[2,3]{1,0:T(2,128)S(1)}, u32[]{:S(2)}, u32[]{:S(2)}) %collective-permute-start) | collective-permute-done | bytes 56 | tf_op jit(solution)/shard_map/ppermute | solution.py:20
  8.1 0.0 copy-start
  8.1 2.2 %copy-done = f32[2,2,256,1024]{3,2,1,0:T(8,128)S(1)} copy-done((f32[2,2,256,1024]{3,2,1,0:T(8,128)S(1)}, f32[2,2,256,1024]{3,2,1,0:T(8,128)}, u32[]{:S(2)}) %copy-start) | copy-done | bytes 4194328
  10.3 0.0 copy-start.1
  10.3 0.7 pack.2
  11.0 2.1 %collective-permute-start.1 = (f32[2,2,256,256]{3,2,1,0:T(8,128)S(1)}, f32[2,2,256,256]{3,2,1,0:T(8,128)S(1)}, u32[]{:S(2)}, u32[]{:S(2)}) collective-permute-start(f32[2,2,256,256]{3,2,1,0:T(8,128)S(1)} %pack.2), channel_id=1, source_target_pairs={{1,0},{2,1},{3,2},{4,3},{5,4},{6,5},{7,6},{8,7},{9,8},{10,9},{11,1... | collective-permute-start | bytes 3145736 | tf_op jit(solution)/shard_map/ppermute | solution.py:20
  13.0 0.0 copy-done.1
  13.0 0.0 copy-start.2
  13.0 0.0 copy-start.3
  13.1 0.7 pack.3
  13.8 2.5 %collective-permute-start.2 = (f32[2,2,256,256]{3,2,1,0:T(8,128)S(1)}, f32[2,2,256,256]{3,2,1,0:T(8,128)S(1)}, u32[]{:S(2)}, u32[]{:S(2)}) collective-permute-start(f32[2,2,256,256]{3,2,1,0:T(8,128)S(1)} %pack.3), channel_id=1, source_target_pairs={{1,0},{2,1},{3,2},{4,3},{5,4},{6,5},{7,6},{8,7},{9,8},{10,9},{11,1... | collective-permute-start | bytes 3145736 | tf_op jit(solution)/shard_map/ppermute | solution.py:20
  16.3 9.0 %collective-permute-done.1.beyond = f32[2,2,256,256]{3,2,1,0:T(8,128)S(1)} collective-permute-done((f32[2,2,256,256]{3,2,1,0:T(8,128)S(1)}, f32[2,2,256,256]{3,2,1,0:T(8,128)S(1)}, u32[]{:S(2)}, u32[]{:S(2)}) %collective-permute-start.1) | collective-permute-done | bytes 1048608 | tf_op jit(solution)/shard_map/ppermute | solution.py:20
  25.3 0.0 copy-done.2
  25.3 0.0 copy-done.3
  25.3 10.5 %position.2.piece0 = f32[2,2,256,256]{3,2,1,0:T(8,128)S(1)} custom-call(s32[3]{0:T(128)S(1)} %get-tuple-element.8.place, f32[2,2,256,1024]{3,2,1,0:T(8,128)} %objects.1, f32[2,2,256,1024]{3,2,1,0:T(8,128)} %objects.1, f32[2,2,256,256]{3,2,1,0:T(8,128)S(1)} %collective-permute-done.1.beyond, f32[2,2,256,256]{3,2,1,0:T(8,128)S(1)} %copy-done.2, ...), custom_call_target="tpu_custom_call" | custom-call | flops 3221225472 | bytes 10485760 | tf_op jit(solution)/shard_map/position/pallas_call | solution.py:157
  35.8 2.8 %collective-permute-start.3 = (f32[2,2,256,256]{3,2,1,0:T(8,128)S(1)}, f32[2,2,256,256]{3,2,1,0:T(8,128)S(1)}, u32[]{:S(2)}, u32[]{:S(2)}) collective-permute-start(f32[2,2,256,256]{3,2,1,0:T(8,128)S(1)} %position.2.piece0), channel_id=1, source_target_pairs={{0,1},{1,2},{2,3},{3,4},{4,5},{5,6},{6,7},{7,8},{8,9},{9,10},{10,1... | collective-permute-start | bytes 3145736 | tf_op jit(solution)/shard_map/ppermute | solution.py:20
  38.7 0.0 collective-permute-done.2.beyond
  38.7 10.5 %position.3.piece1 = f32[2,2,256,256]{3,2,1,0:T(8,128)S(1)} custom-call(s32[3]{0:T(128)S(1)} %get-tuple-element.7.place, f32[2,2,256,1024]{3,2,1,0:T(8,128)} %objects.1, f32[2,2,256,1024]{3,2,1,0:T(8,128)} %objects.1, f32[2,2,256,256]{3,2,1,0:T(8,128)S(1)} %collective-permute-done.2.beyond, f32[2,2,256,256]{3,2,1,0:T(8,128)S(1)} %copy-done.2, ...), custom_call_target="tpu_custom_call" | custom-call | flops 3221225472 | bytes 10485760 | tf_op jit(solution)/shard_map/position/pallas_call | solution.py:157
  49.2 1.9 %collective-permute-start.4 = (f32[2,2,256,256]{3,2,1,0:T(8,128)S(1)}, f32[2,2,256,256]{3,2,1,0:T(8,128)S(1)}, u32[]{:S(2)}, u32[]{:S(2)}) collective-permute-start(f32[2,2,256,256]{3,2,1,0:T(8,128)S(1)} %position.3.piece1), channel_id=1, source_target_pairs={{0,1},{1,2},{2,3},{3,4},{4,5},{5,6},{6,7},{7,8},{8,9},{9,10},{10,1... | collective-permute-start | bytes 3145736 | tf_op jit(solution)/shard_map/ppermute | solution.py:20
  51.1 0.1 pad_add_fusion.places
  51.2 1.8 %collective-permute-done.3.back0 = f32[2,2,256,256]{3,2,1,0:T(8,128)S(1)} collective-permute-done((f32[2,2,256,256]{3,2,1,0:T(8,128)S(1)}, f32[2,2,256,256]{3,2,1,0:T(8,128)S(1)}, u32[]{:S(2)}, u32[]{:S(2)}) %collective-permute-start.3) | collective-permute-done | bytes 1048608 | tf_op jit(solution)/shard_map/ppermute | solution.py:20
  53.0 13.2 %collective-permute-done.4.back1 = f32[2,2,256,256]{3,2,1,0:T(8,128)S(1)} collective-permute-done((f32[2,2,256,256]{3,2,1,0:T(8,128)S(1)}, f32[2,2,256,256]{3,2,1,0:T(8,128)S(1)}, u32[]{:S(2)}, u32[]{:S(2)}) %collective-permute-start.4) | collective-permute-done | bytes 1048608 | tf_op jit(solution)/shard_map/ppermute | solution.py:20
  66.2 6.4 %update.1 = f32[2,2,256,1024]{3,2,1,0:T(8,128)} custom-call(s32[4,3]{1,0:T(4,128)S(1)} %pad_add_fusion.places, f32[2,2,256,1024]{3,2,1,0:T(8,128)} %objects.1, f32[2,2,256,256]{3,2,1,0:T(8,128)S(1)} %position.2.piece0, f32[2,2,256,256]{3,2,1,0:T(8,128)S(1)} %position.3.piece1, f32[2,2,256,256]{3,2,1,0:T(8,128)S(1)} %collective-permute-done.3.back0, ...), custom_call_target="tpu_custom_call" | custom-call | tf_op jit(solution)/shard_map/update/pallas_call | solution.py:187
  (2 shorter events, 0.0 us)
Async XLA Ops:
  2.3 5.8 %collective-permute-start = (s32[2,3]{1,0:T(2,128)S(1)}, s32[2,3]{1,0:T(2,128)S(1)}, u32[]{:S(2)}, u32[]{:S(2)}) collective-permute-start(s32[2,3]{1,0:T(2,128)S(1)} %pad_add_fusion.1), channel_id=1, source_target_pairs={{0,1},{1,2},{2,3},{3,4},{4,5},{5,6},{6,7},{7,8},{8,9},{9,10},{10,1... | collective-permute-start | bytes 80 | tf_op jit(solution)/shard_map/ppermute | solution.py:20
  8.1 2.2 %copy-start = (f32[2,2,256,1024]{3,2,1,0:T(8,128)S(1)}, f32[2,2,256,1024]{3,2,1,0:T(8,128)}, u32[]{:S(2)}) copy-start(f32[2,2,256,1024]{3,2,1,0:T(8,128)} %objects.1) | copy-start | bytes 12582916
  10.3 2.8 %copy-start.1 = (f32[2,2,256,1024]{3,2,1,0:T(8,128)S(1)}, f32[2,2,256,1024]{3,2,1,0:T(8,128)}, u32[]{:S(2)}) copy-start(f32[2,2,256,1024]{3,2,1,0:T(8,128)} %objects.1) | copy-start | bytes 12582916
  11.0 14.4 %collective-permute-start.1 = (f32[2,2,256,256]{3,2,1,0:T(8,128)S(1)}, f32[2,2,256,256]{3,2,1,0:T(8,128)S(1)}, u32[]{:S(2)}, u32[]{:S(2)}) collective-permute-start(f32[2,2,256,256]{3,2,1,0:T(8,128)S(1)} %pack.2), channel_id=1, source_target_pairs={{1,0},{2,1},{3,2},{4,3},{5,4},{6,5},{7,6},{8,7},{9,8},{10,9},{11,1... | collective-permute-start | bytes 3145736 | tf_op jit(solution)/shard_map/ppermute | solution.py:20
  13.0 12.3 %copy-start.2 = (f32[2,2,256,256]{3,2,1,0:T(8,128)S(1)}, f32[2,2,256,256]{3,2,1,0:T(8,128)}, u32[]{:S(2)}) copy-start(f32[2,2,256,256]{3,2,1,0:T(8,128)} %probe.3) | copy-start | bytes 3145732
  13.0 12.3 %copy-start.3 = (f32[2,256,256]{2,1,0:T(8,128)S(1)}, f32[2,256,256]{2,1,0:T(8,128)}, u32[]{:S(2)}) copy-start(f32[2,256,256]{2,1,0:T(8,128)} %measured.3) | copy-start | bytes 1572868
  13.8 24.9 %collective-permute-start.2 = (f32[2,2,256,256]{3,2,1,0:T(8,128)S(1)}, f32[2,2,256,256]{3,2,1,0:T(8,128)S(1)}, u32[]{:S(2)}, u32[]{:S(2)}) collective-permute-start(f32[2,2,256,256]{3,2,1,0:T(8,128)S(1)} %pack.3), channel_id=1, source_target_pairs={{1,0},{2,1},{3,2},{4,3},{5,4},{6,5},{7,6},{8,7},{9,8},{10,9},{11,1... | collective-permute-start | bytes 3145736 | tf_op jit(solution)/shard_map/ppermute | solution.py:20
  35.8 17.2 %collective-permute-start.3 = (f32[2,2,256,256]{3,2,1,0:T(8,128)S(1)}, f32[2,2,256,256]{3,2,1,0:T(8,128)S(1)}, u32[]{:S(2)}, u32[]{:S(2)}) collective-permute-start(f32[2,2,256,256]{3,2,1,0:T(8,128)S(1)} %position.2.piece0), channel_id=1, source_target_pairs={{0,1},{1,2},{2,3},{3,4},{4,5},{5,6},{6,7},{7,8},{8,9},{9,10},{10,1... | collective-permute-start | bytes 3145736 | tf_op jit(solution)/shard_map/ppermute | solution.py:20
  49.2 17.0 %collective-permute-start.4 = (f32[2,2,256,256]{3,2,1,0:T(8,128)S(1)}, f32[2,2,256,256]{3,2,1,0:T(8,128)S(1)}, u32[]{:S(2)}, u32[]{:S(2)}) collective-permute-start(f32[2,2,256,256]{3,2,1,0:T(8,128)S(1)} %position.3.piece1), channel_id=1, source_target_pairs={{0,1},{1,2},{2,3},{3,4},{4,5},{5,6},{6,7},{7,8},{8,9},{9,10},{10,1... | collective-permute-start | bytes 3145736 | tf_op jit(solution)/shard_map/ppermute | solution.py:20

commit v2 on v0

v2 whole, which is shorter than its diff:
```python
import jax
import jax.numpy as jnp
import numpy as np
from jax import lax
from jax.experimental import pallas as pl
from jax.experimental.pallas import tpu as pltpu
from jax.sharding import PartitionSpec as P

spread_phase = 40.0
descent_rate = 1.0
VMEM_BYTES = 60 * 1024 * 1024


def tables(width):
    counter = np.arange(width)
    fourier = np.exp(-2j * np.pi * (np.outer(counter, counter) % width) / width) / np.sqrt(width)
    folded = ((counter + width // 2) % width - width // 2) / width
    phase = np.exp(-1j * spread_phase * folded**2)
    moving = np.conj(fourier) @ (phase[:, None] * fourier)
    parts = [[matrix.real, matrix.imag] for matrix in (moving, fourier)]
    return np.array(parts, dtype=np.float32)


def halves(values):
    high = values.astype(jnp.bfloat16)
    low = (values - high.astype(jnp.float32)).astype(jnp.bfloat16)
    return high, low


def transform(real, imag, right, left):
    width = real.shape[0]
    high, low = halves(jnp.concatenate([real, imag], axis=1))
    rows = jnp.dot(
        jnp.concatenate([high, low, high], axis=1), right, preferred_element_type=jnp.float32
    )
    high, low = halves(jnp.concatenate([rows[:, :width], rows[:, width:]], axis=0))
    both = jnp.dot(
        left, jnp.concatenate([high, low, high], axis=0), preferred_element_type=jnp.float32
    )
    return both[:width], both[width:]


def times(a, b):
    return a[0] * b[0] - a[1] * b[1], a[0] * b[1] + a[1] * b[0]


def kernel(
    x_ref,
    y_ref,
    mode_ref,
    objects_hbm,
    probes_hbm,
    measured_hbm,
    tables_hbm,
    updated_hbm,
    objects,
    probes,
    measured,
    tables_f32,
    right,
    left,
    total,
    place,
    place_before,
    packed,
    beyond,
    pieces,
    returned,
    load_sem,
    place_sem,
    object_sem,
    piece_sem,
    store_sem,
):
    slices, _, tile, span = objects.shape
    amount, width, _ = measured.shape
    me, devices = lax.axis_index("lat"), lax.axis_size("lat")
    has_before, has_after = me > 0, me < devices - 1
    before, after = jnp.maximum(me - 1, 0), jnp.minimum(me + 1, devices - 1)

    def send(source, target, sems, towards):
        return pltpu.make_async_remote_copy(
            src_ref=source,
            dst_ref=target,
            send_sem=sems[0],
            recv_sem=sems[1],
            device_id={"lat": towards},
            device_id_type=pl.DeviceIdType.MESH,
        )

    def send_place():
        return send(place, place_before, (place_sem.at[0], place_sem.at[1]), after)

    def send_objects(p, s):
        sems = (object_sem.at[0, p, s], object_sem.at[1, p, s])
        return send(packed.at[p, s], beyond.at[p, s], sems, before)

    def send_piece(p, s):
        sems = (piece_sem.at[0, p, s], piece_sem.at[1, p, s])
        return send(pieces.at[p, s], returned.at[p, s], sems, after)

    load_objects = pltpu.make_async_copy(objects_hbm, objects, load_sem.at[0])
    others = [
        pltpu.make_async_copy(source, target, load_sem.at[i + 1])
        for i, (source, target) in enumerate(
            [(tables_hbm, tables_f32), (probes_hbm, probes), (measured_hbm, measured)]
        )
    ]
    load_objects.start()
    for p in range(amount):
        place[p] = jnp.full((1, width), x_ref[p], jnp.int32)
        place[amount + p] = jnp.full((1, width), y_ref[p], jnp.int32)

    barrier = pltpu.get_barrier_semaphore()

    @pl.when(has_before)
    def _():
        pl.semaphore_signal(
            barrier, inc=1, device_id={"lat": before}, device_id_type=pl.DeviceIdType.MESH
        )

    @pl.when(has_after)
    def _():
        pl.semaphore_signal(
            barrier, inc=1, device_id={"lat": after}, device_id_type=pl.DeviceIdType.MESH
        )

    peers = has_before.astype(jnp.int32) + has_after.astype(jnp.int32)
    pl.semaphore_wait(barrier, peers)

    @pl.when(has_after)
    def _():
        send_place().start()

    row = lax.broadcasted_iota(jnp.int32, (width, width), 0)
    column = lax.broadcasted_iota(jnp.int32, (width, width), 1)

    def across(y, k):
        return (column + k * width >= y) & (column + k * width < y + width)

    def gathered(y, s, c):
        value = objects[s, c, :, 0:width]
        for k in range(1, span // width):
            value = jnp.where(across(y, k), objects[s, c, :, k * width : (k + 1) * width], value)
        return value

    load_objects.wait()

    @pl.when(has_before)
    def _():
        send_place().wait_recv()

        def pack(p, carry):
            y = place_before[amount + p]
            for s in range(slices):
                for c in range(2):
                    packed[p, s, c] = gathered(y, s, c)
                send_objects(p, s).start()
            return carry

        lax.fori_loop(0, amount, pack, 0)

    for copy in others:
        copy.start()

    @pl.when(jnp.logical_not(has_after))
    def _():
        beyond[...] = jnp.zeros_like(beyond)

    for copy in others:
        copy.wait()

    for i in range(2):
        for c, sign in ((0, 1.0), (1, 1.0), (1, -1.0)):
            high, low = halves(sign * tables_f32[i, c])
            for k, part in enumerate((high, high, low)):
                base = 2 * width * k
                near, further = pl.ds(base, width), pl.ds(base + width, width)
                first, second = pl.ds(0, width), pl.ds(width, width)
                if c == 0:
                    right[i, near, first] = part
                    right[i, further, second] = part
                    left[i, first, near] = part
                    left[i, second, further] = part
                elif sign > 0:
                    right[i, near, second] = part
                    left[i, second, near] = part
                else:
                    right[i, further, first] = part
                    left[i, first, further] = part

    def visit(p, carry):
        x, y, mode = x_ref[p], y_ref[p], mode_ref[p]
        inside = row >= x
        shift = lax.rem(y, width)
        entry = [pltpu.roll(pltpu.roll(probes[mode, c], x, 0), shift, 1) for c in range(2)]

        def window(s):
            own = [gathered(y, s, c) for c in range(2)]

            @pl.when(has_after)
            def _():
                send_objects(p, s).wait_recv()

            return [jnp.where(inside, own[c], beyond[p, s, c]) for c in range(2)]

        def emit(s, piece):
            pieces[p, s, 0] = piece[0]
            pieces[p, s, 1] = -piece[1]

            @pl.when(has_after)
            def _():
                send_piece(p, s).start()

        move, far = (right[0], left[0]), (right[1], left[1])
        middle = transform(*times(entry, window(0)), *move)
        slab = window(1)
        psi = transform(*times(middle, slab), *far)
        residual = psi[0] * psi[0] + psi[1] * psi[1] - measured[p]
        back = transform(residual * psi[0], -(residual * psi[1]), *far)
        emit(1, times(middle, back))
        back = transform(*times(slab, back), *move)
        emit(0, times(entry, back))
        return carry

    lax.fori_loop(0, amount, visit, 0)

    def own_update(s, carry):
        for c in range(2):
            for k in range(span // width):
                value = objects[s, c, :, k * width : (k + 1) * width]
                for p in range(amount):
                    mask = across(y_ref[p], k) & (row >= x_ref[p])
                    value = value - descent_rate * jnp.where(mask, pieces[p, s, c], 0.0)
                total[s, c, :, k * width : (k + 1) * width] = value
        return carry

    lax.fori_loop(0, slices, own_update, 0)

    def store(s):
        return pltpu.make_async_copy(total.at[s], updated_hbm.at[s], store_sem.at[s])

    def late_update(step, carry):
        p, s = step // slices, slices - 1 - step % slices

        @pl.when(has_before)
        def _():
            send_piece(p, s).wait_recv()
            x, y = place_before[p], place_before[amount + p]
            inside = row < x
            for c in range(2):
                piece = jnp.where(inside, returned[p, s, c], 0.0)
                for k in range(span // width):
                    kept = jnp.where(across(y, k), piece, 0.0)
                    where = (s, c, slice(None), slice(k * width, (k + 1) * width))
                    total[where] = total[where] - descent_rate * kept

        @pl.when(p == amount - 1)
        def _():
            store(s).start()

        return carry

    lax.fori_loop(0, amount * slices, late_update, 0)

    for p in range(amount):
        for s in range(slices):

            @pl.when(has_before)
            def _():
                send_objects(p, s).wait_send()

            @pl.when(has_after)
            def _():
                send_piece(p, s).wait_send()

    @pl.when(has_after)
    def _():
        send_place().wait_send()

    for s in range(slices):
        store(s).wait()


def on_device(objects, probes, x_offsets, y_offsets, modes, measured):
    slices = objects.shape[0]
    amount, width, _ = measured.shape
    factors = jnp.asarray(tables(width))
    windows = (amount, slices, 2, width, width)
    small = pl.BlockSpec(memory_space=pltpu.SMEM)
    large = pl.BlockSpec(memory_space=pl.ANY)
    return pl.pallas_call(
        kernel,
        out_shape=jax.ShapeDtypeStruct(objects.shape, jnp.float32),
        in_specs=[small] * 3 + [large] * 4,
        out_specs=large,
        scratch_shapes=[
            pltpu.VMEM(objects.shape, jnp.float32),
            pltpu.VMEM(probes.shape, jnp.float32),
            pltpu.VMEM(measured.shape, jnp.float32),
            pltpu.VMEM(factors.shape, jnp.float32),
            pltpu.VMEM((2, 6 * width, 2 * width), jnp.bfloat16),
            pltpu.VMEM((2, 2 * width, 6 * width), jnp.bfloat16),
            pltpu.VMEM(objects.shape, jnp.float32),
            pltpu.VMEM((2 * amount, 1, width), jnp.int32),
            pltpu.VMEM((2 * amount, 1, width), jnp.int32),
            pltpu.VMEM(windows, jnp.float32),
            pltpu.VMEM(windows, jnp.float32),
            pltpu.VMEM(windows, jnp.float32),
            pltpu.VMEM(windows, jnp.float32),
            pltpu.SemaphoreType.DMA((4,)),
            pltpu.SemaphoreType.DMA((2,)),
            pltpu.SemaphoreType.DMA((2, amount, slices)),
            pltpu.SemaphoreType.DMA((2, amount, slices)),
            pltpu.SemaphoreType.DMA((slices,)),
        ],
        compiler_params=pltpu.CompilerParams(
            collective_id=0, has_side_effects=True, vmem_limit_bytes=VMEM_BYTES
        ),
        cost_estimate=pl.CostEstimate(
            flops=amount * 8 * 2 * 6 * 2 * width**3, bytes_accessed=16 << 20, transcendentals=0
        ),
        name="gradient_step",
    )(x_offsets, y_offsets, modes, objects, probes, measured, factors)


def solution(mesh):
    in_specs = (
        P(None, None, ("groups", "lat"), None),
        P("groups", None, None, None),
        P(("groups", "lat")),
        P(("groups", "lat")),
        P(("groups", "lat")),
        P(("groups", "lat"), None, None),
    )
    out_specs = P(None, None, ("groups", "lat"), None)
    return jax.shard_map(
        on_device, mesh=mesh, in_specs=in_specs, out_specs=out_specs, check_vma=False
    )
```

time: 272 us -> 76 us (0.28)
  the two profiles are of different devices: /device:TPU:8 before, /device:TPU:12 now
where the time goes in v2:
time: 76 us; the launch traced here: 75.8 us
  Pallas kernels  71 us (93%)
  local copies, waits for them, and re-layouts  4.79 us (6%)
    pallas_call x1, Pallas kernels, on_device(): pl.pallas_call(kernel, out_shape=jax.ShapeDtypeStruct(objects.shape, jnp....  71 us
    unnamed x1, local copies, waits for them, and re-layouts  4.79 us

profile of v2, /device:TPU:12, one launch (start us, length us, event | category | flops | bytes accessed | tf_op | source)
XLA Modules:
  0.0 75.8 jit_solution(14575013509266291670)
XLA Ops:
  0.0 71.0 %gradient_step.1 = f32[2,2,256,1024]{3,2,1,0:T(8,128)} custom-call(s32[2]{0:T(128)} %x_ref.1, s32[2]{0:T(128)} %y_ref.1, s32[2]{0:T(128)} %mode_ref.1, f32[2,2,256,1024]{3,2,1,0:T(8,128)} %objects_hbm.1, f32[2,2,256,256]{3,2,1,0:T(8,128)} %probes_hbm.1, f32[2,256,256]{2,1,0:T(8,128)} %measured_hbm.1, f32[2,2,256,256]{3,2,1,0:T(8,128)} %constant.2.clone.tables_hbm), custom_call_target="tpu_custom_call" | custom-call | flops 6442450944 | bytes 16777216 | tf_op jit(solution)/shard_map/gradient_step/pallas_call | solution.py:292
  71.0 4.8 %copy.9 = f32[2,2,256,1024]{3,2,1,0:T(8,128)} copy(f32[2,2,256,1024]{3,2,1,0:T(8,128)} %gradient_step.1) | data formatting | bytes 8388608

commit v3 on v2

--- a/solution.py
+++ b/solution.py
@@ -8,7 +8,7 @@
 
 spread_phase = 40.0
 descent_rate = 1.0
-VMEM_BYTES = 60 * 1024 * 1024
+VMEM_BYTES = 59 * 1024 * 1024
 
 
 def tables(width):
@@ -155,7 +155,11 @@
             for s in range(slices):
                 for c in range(2):
                     packed[p, s, c] = gathered(y, s, c)
-                send_objects(p, s).start()
+
+                @pl.when(p == 0)
+                def _():
+                    send_objects(p, s).start()
+
             return carry
 
         lax.fori_loop(0, amount, pack, 0)
@@ -190,6 +194,12 @@
                     left[i, first, further] = part
 
     def visit(p, carry):
+        @pl.when(has_before & (p + 1 < amount))
+        def _():
+            for s in range(slices):
+                send_objects(p, s).wait_send()
+                send_objects(p + 1, s).start()
+
         x, y, mode = x_ref[p], y_ref[p], mode_ref[p]
         inside = row >= x
         shift = lax.rem(y, width)
@@ -263,12 +273,13 @@
 
     lax.fori_loop(0, amount * slices, late_update, 0)
 
-    for p in range(amount):
-        for s in range(slices):
-
-            @pl.when(has_before)
-            def _():
-                send_objects(p, s).wait_send()
+    for s in range(slices):
+
+        @pl.when(has_before)
+        def _():
+            send_objects(amount - 1, s).wait_send()
+
+        for p in range(amount):
 
             @pl.when(has_after)
             def _():
@@ -288,12 +299,12 @@
     factors = jnp.asarray(tables(width))
     windows = (amount, slices, 2, width, width)
     small = pl.BlockSpec(memory_space=pltpu.SMEM)
-    large = pl.BlockSpec(memory_space=pl.ANY)
+    large = pl.BlockSpec(memory_space=pltpu.HBM)
     return pl.pallas_call(
         kernel,
-        out_shape=jax.ShapeDtypeStruct(objects.shape, jnp.float32),
+        out_shape=pltpu.VMEM(objects.shape, jnp.float32),
         in_specs=[small] * 3 + [large] * 4,
-        out_specs=large,
+        out_specs=pl.BlockSpec(memory_space=pl.ANY),
         scratch_shapes=[
             pltpu.VMEM(objects.shape, jnp.float32),
             pltpu.VMEM(probes.shape, jnp.float32),

time: 76 us -> 72 us (0.947)
  the two profiles are of different devices: /device:TPU:12 before, /device:TPU:20 now
where the time goes in v3:
time: 72 us; the launch traced here: 71.9 us
  Pallas kernels  69.8 us (97%)
  local copies, waits for them, and re-layouts  2.02 us (3%)
    pallas_call x1, Pallas kernels, on_device(): pl.pallas_call(kernel, out_shape=pltpu.VMEM(objects.shape, jnp.float32),...  69.8 us
    unnamed x1, local copies, waits for them, and re-layouts  2.02 us

profile of v3, /device:TPU:20, one launch (start us, length us, event | category | flops | bytes accessed | tf_op | source)
XLA Modules:
  0.0 71.9 jit_solution(14529585275776436112)
XLA Ops:
  0.0 69.8 %gradient_step.1 = f32[2,2,256,1024]{3,2,1,0:T(8,128)S(1)} custom-call(s32[2]{0:T(128)} %x_ref.1, s32[2]{0:T(128)} %y_ref.1, s32[2]{0:T(128)} %mode_ref.1, f32[2,2,256,1024]{3,2,1,0:T(8,128)} %objects_hbm.1, f32[2,2,256,256]{3,2,1,0:T(8,128)} %probes_hbm.1, f32[2,256,256]{2,1,0:T(8,128)} %measured_hbm.1, f32[2,2,256,256]{3,2,1,0:T(8,128)} %constant.2.clone.tables_hbm), custom_call_target="tpu_custom_call" | custom-call | flops 6442450944 | bytes 16777216 | tf_op jit(solution)/shard_map/gradient_step/pallas_call | solution.py:303
  69.8 2.0 %copy.9 = f32[2,2,256,1024]{3,2,1,0:T(8,128)} copy(f32[2,2,256,1024]{3,2,1,0:T(8,128)S(1)} %gradient_step.1) | data formatting | bytes 8388608

commit v4 on v3

--- a/solution.py
+++ b/solution.py
@@ -218,13 +218,19 @@
             pieces[p, s, 0] = piece[0]
             pieces[p, s, 1] = -piece[1]
 
-            @pl.when(has_after)
+            @pl.when(has_after & (p == amount - 1))
             def _():
                 send_piece(p, s).start()
 
         move, far = (right[0], left[0]), (right[1], left[1])
         middle = transform(*times(entry, window(0)), *move)
         slab = window(1)
+
+        @pl.when(has_after & (p > 0))
+        def _():
+            for s in reversed(range(slices)):
+                send_piece(p - 1, s).start()
+
         psi = transform(*times(middle, slab), *far)
         residual = psi[0] * psi[0] + psi[1] * psi[1] - measured[p]
         back = transform(residual * psi[0], -(residual * psi[1]), *far)

time: 72 us -> 59.3 us (0.82)
  the two profiles are of different devices: /device:TPU:20 before, /device:TPU:8 now
where the time goes in v4:
time: 59.3 us; the launch traced here: 59.1 us
  Pallas kernels  57.1 us (96%)
  local copies, waits for them, and re-layouts  2.02 us (3%)
    pallas_call x1, Pallas kernels, on_device(): pl.pallas_call(kernel, out_shape=pltpu.VMEM(objects.shape, jnp.float32),...  57.1 us
    unnamed x1, local copies, waits for them, and re-layouts  2.02 us

profile of v4, /device:TPU:8, one launch (start us, length us, event | category | flops | bytes accessed | tf_op | source)
XLA Modules:
  0.0 59.1 jit_solution(10818197867148481021)
XLA Ops:
  0.0 57.1 %gradient_step.1 = f32[2,2,256,1024]{3,2,1,0:T(8,128)S(1)} custom-call(s32[2]{0:T(128)} %x_ref.1, s32[2]{0:T(128)} %y_ref.1, s32[2]{0:T(128)} %mode_ref.1, f32[2,2,256,1024]{3,2,1,0:T(8,128)} %objects_hbm.1, f32[2,2,256,256]{3,2,1,0:T(8,128)} %probes_hbm.1, f32[2,256,256]{2,1,0:T(8,128)} %measured_hbm.1, f32[2,2,256,256]{3,2,1,0:T(8,128)} %constant.2.clone.tables_hbm), custom_call_target="tpu_custom_call" | custom-call | flops 6442450944 | bytes 16777216 | tf_op jit(solution)/shard_map/gradient_step/pallas_call | solution.py:309
  57.1 2.0 %copy.9 = f32[2,2,256,1024]{3,2,1,0:T(8,128)} copy(f32[2,2,256,1024]{3,2,1,0:T(8,128)S(1)} %gradient_step.1) | data formatting | bytes 8388608

commit v5 on v3

--- a/solution.py
+++ b/solution.py
@@ -52,25 +52,24 @@
     probes_hbm,
     measured_hbm,
     tables_hbm,
-    updated_hbm,
+    total,
     objects,
     probes,
     measured,
     tables_f32,
     right,
     left,
-    total,
     place,
     place_before,
     packed,
     beyond,
     pieces,
     returned,
+    object_load_sem,
     load_sem,
     place_sem,
     object_sem,
     piece_sem,
-    store_sem,
 ):
     slices, _, tile, span = objects.shape
     amount, width, _ = measured.shape
@@ -99,14 +98,18 @@
         sems = (piece_sem.at[0, p, s], piece_sem.at[1, p, s])
         return send(pieces.at[p, s], returned.at[p, s], sems, after)
 
-    load_objects = pltpu.make_async_copy(objects_hbm, objects, load_sem.at[0])
+    load_objects = [
+        pltpu.make_async_copy(objects_hbm.at[s], objects.at[s], object_load_sem.at[s])
+        for s in range(slices)
+    ]
     others = [
-        pltpu.make_async_copy(source, target, load_sem.at[i + 1])
+        pltpu.make_async_copy(source, target, load_sem.at[i])
         for i, (source, target) in enumerate(
             [(tables_hbm, tables_f32), (probes_hbm, probes), (measured_hbm, measured)]
         )
     ]
-    load_objects.start()
+    for copy in load_objects:
+        copy.start()
     for p in range(amount):
         place[p] = jnp.full((1, width), x_ref[p], jnp.int32)
         place[amount + p] = jnp.full((1, width), y_ref[p], jnp.int32)
@@ -144,25 +147,22 @@
             value = jnp.where(across(y, k), objects[s, c, :, k * width : (k + 1) * width], value)
         return value
 
-    load_objects.wait()
-
     @pl.when(has_before)
     def _():
         send_place().wait_recv()
 
-        def pack(p, carry):
-            y = place_before[amount + p]
-            for s in range(slices):
+    for p in range(amount):
+        for s in range(slices):
+            if p == 0:
+                load_objects[s].wait()
+
+            @pl.when(has_before)
+            def _():
+                y = place_before[amount + p]
                 for c in range(2):
                     packed[p, s, c] = gathered(y, s, c)
-
-                @pl.when(p == 0)
-                def _():
+                if p == 0:
                     send_objects(p, s).start()
-
-            return carry
-
-        lax.fori_loop(0, amount, pack, 0)
 
     for copy in others:
         copy.start()
@@ -205,22 +205,29 @@
         shift = lax.rem(y, width)
         entry = [pltpu.roll(pltpu.roll(probes[mode, c], x, 0), shift, 1) for c in range(2)]
 
+        @pl.when(has_after)
+        def _():
+            for s in range(slices):
+                send_objects(p, s).wait_recv()
+
+        @pl.when(has_after & (p > 0))
+        def _():
+            for s in reversed(range(slices)):
+                send_piece(p - 1, s).start()
+
         def window(s):
             own = [gathered(y, s, c) for c in range(2)]
-
-            @pl.when(has_after)
-            def _():
-                send_objects(p, s).wait_recv()
-
             return [jnp.where(inside, own[c], beyond[p, s, c]) for c in range(2)]
 
         def emit(s, piece):
             pieces[p, s, 0] = piece[0]
             pieces[p, s, 1] = -piece[1]
 
-            @pl.when(has_after)
-            def _():
-                send_piece(p, s).start()
+            if s > 0 or amount == 1:
+
+                @pl.when(has_after & (p == amount - 1))
+                def _():
+                    send_piece(p, s).start()
 
         move, far = (right[0], left[0]), (right[1], left[1])
         middle = transform(*times(entry, window(0)), *move)
@@ -247,8 +254,13 @@
 
     lax.fori_loop(0, slices, own_update, 0)
 
-    def store(s):
-        return pltpu.make_async_copy(total.at[s], updated_hbm.at[s], store_sem.at[s])
+    if amount > 1:
+
+        @pl.when(has_after)
+        def _():
+            for s in reversed(range(slices)):
+                send_piece(amount - 2, s).wait_send()
+            send_piece(amount - 1, 0).start()
 
     def late_update(step, carry):
         p, s = step // slices, slices - 1 - step % slices
@@ -265,10 +277,6 @@
                     where = (s, c, slice(None), slice(k * width, (k + 1) * width))
                     total[where] = total[where] - descent_rate * kept
 
-        @pl.when(p == amount - 1)
-        def _():
-            store(s).start()
-
         return carry
 
     lax.fori_loop(0, amount * slices, late_update, 0)
@@ -280,17 +288,15 @@
             send_objects(amount - 1, s).wait_send()
 
         for p in range(amount):
-
-            @pl.when(has_after)
-            def _():
-                send_piece(p, s).wait_send()
+            if p != amount - 2:
+
+                @pl.when(has_after)
+                def _():
+                    send_piece(p, s).wait_send()
 
     @pl.when(has_after)
     def _():
         send_place().wait_send()
-
-    for s in range(slices):
-        store(s).wait()
 
 
 def on_device(objects, probes, x_offsets, y_offsets, modes, measured):
@@ -304,7 +310,7 @@
         kernel,
         out_shape=pltpu.VMEM(objects.shape, jnp.float32),
         in_specs=[small] * 3 + [large] * 4,
-        out_specs=pl.BlockSpec(memory_space=pl.ANY),
+        out_specs=pl.BlockSpec(memory_space=pltpu.VMEM),
         scratch_shapes=[
             pltpu.VMEM(objects.shape, jnp.float32),
             pltpu.VMEM(probes.shape, jnp.float32),
@@ -312,18 +318,17 @@
             pltpu.VMEM(factors.shape, jnp.float32),
             pltpu.VMEM((2, 6 * width, 2 * width), jnp.bfloat16),
             pltpu.VMEM((2, 2 * width, 6 * width), jnp.bfloat16),
-            pltpu.VMEM(objects.shape, jnp.float32),
             pltpu.VMEM((2 * amount, 1, width), jnp.int32),
             pltpu.VMEM((2 * amount, 1, width), jnp.int32),
             pltpu.VMEM(windows, jnp.float32),
             pltpu.VMEM(windows, jnp.float32),
             pltpu.VMEM(windows, jnp.float32),
             pltpu.VMEM(windows, jnp.float32),
-            pltpu.SemaphoreType.DMA((4,)),
+            pltpu.SemaphoreType.DMA((slices,)),
+            pltpu.SemaphoreType.DMA((3,)),
             pltpu.SemaphoreType.DMA((2,)),
             pltpu.SemaphoreType.DMA((2, amount, slices)),
             pltpu.SemaphoreType.DMA((2, amount, slices)),
-            pltpu.SemaphoreType.DMA((slices,)),
         ],
         compiler_params=pltpu.CompilerParams(
             collective_id=0, has_side_effects=True, vmem_limit_bytes=VMEM_BYTES

time: 72 us -> 57.5 us (0.80)
  the two profiles are of different devices: /device:TPU:20 before, /device:TPU:8 now
where the time goes in v5:
time: 57.5 us; the launch traced here: 57.3 us
  Pallas kernels  55.3 us (96%)
  local copies, waits for them, and re-layouts  2.02 us (4%)
    pallas_call x1, Pallas kernels, on_device(): pl.pallas_call(kernel, out_shape=pltpu.VMEM(objects.shape, jnp.float32),...  55.3 us
    unnamed x1, local copies, waits for them, and re-layouts  2.02 us

profile of v5, /device:TPU:8, one launch (start us, length us, event | category | flops | bytes accessed | tf_op | source)
XLA Modules:
  0.0 57.3 jit_solution(4989965102778451418)
XLA Ops:
  0.0 55.3 %gradient_step.1 = f32[2,2,256,1024]{3,2,1,0:T(8,128)S(1)} custom-call(s32[2]{0:T(128)} %x_ref.1, s32[2]{0:T(128)} %y_ref.1, s32[2]{0:T(128)} %mode_ref.1, f32[2,2,256,1024]{3,2,1,0:T(8,128)} %objects_hbm.1, f32[2,2,256,256]{3,2,1,0:T(8,128)} %probes_hbm.1, f32[2,256,256]{2,1,0:T(8,128)} %measured_hbm.1, f32[2,2,256,256]{3,2,1,0:T(8,128)} %constant.2.clone.tables_hbm), custom_call_target="tpu_custom_call" | custom-call | flops 6442450944 | bytes 16777216 | tf_op jit(solution)/shard_map/gradient_step/pallas_call | solution.py:309
  55.3 2.0 %copy.9 = f32[2,2,256,1024]{3,2,1,0:T(8,128)} copy(f32[2,2,256,1024]{3,2,1,0:T(8,128)S(1)} %gradient_step.1) | data formatting | bytes 8388608

commit v6 on v5

--- a/solution.py
+++ b/solution.py
@@ -45,14 +45,17 @@
 
 
 def kernel(
-    x_ref,
-    y_ref,
-    mode_ref,
+    x_hbm,
+    y_hbm,
+    mode_hbm,
     objects_hbm,
     probes_hbm,
     measured_hbm,
     tables_hbm,
     total,
+    x_ref,
+    y_ref,
+    mode_ref,
     objects,
     probes,
     measured,
@@ -65,6 +68,7 @@
     beyond,
     pieces,
     returned,
+    scalar_sem,
     object_load_sem,
     load_sem,
     place_sem,
@@ -108,25 +112,35 @@
             [(tables_hbm, tables_f32), (probes_hbm, probes), (measured_hbm, measured)]
         )
     ]
+    load_scalars = [
+        pltpu.make_async_copy(source, target, scalar_sem.at[i])
+        for i, (source, target) in enumerate(
+            [(x_hbm, x_ref), (y_hbm, y_ref), (mode_hbm, mode_ref)]
+        )
+    ]
+    for copy in load_scalars:
+        copy.start()
+    barrier = pltpu.get_barrier_semaphore()
+
+    @pl.when(has_before)
+    def _():
+        pl.semaphore_signal(
+            barrier, inc=1, device_id={"lat": before}, device_id_type=pl.DeviceIdType.MESH
+        )
+
+    @pl.when(has_after)
+    def _():
+        pl.semaphore_signal(
+            barrier, inc=1, device_id={"lat": after}, device_id_type=pl.DeviceIdType.MESH
+        )
+
     for copy in load_objects:
         copy.start()
+    for copy in load_scalars:
+        copy.wait()
     for p in range(amount):
         place[p] = jnp.full((1, width), x_ref[p], jnp.int32)
         place[amount + p] = jnp.full((1, width), y_ref[p], jnp.int32)
-
-    barrier = pltpu.get_barrier_semaphore()
-
-    @pl.when(has_before)
-    def _():
-        pl.semaphore_signal(
-            barrier, inc=1, device_id={"lat": before}, device_id_type=pl.DeviceIdType.MESH
-        )
-
-    @pl.when(has_after)
-    def _():
-        pl.semaphore_signal(
-            barrier, inc=1, device_id={"lat": after}, device_id_type=pl.DeviceIdType.MESH
-        )
 
     peers = has_before.astype(jnp.int32) + has_after.astype(jnp.int32)
     pl.semaphore_wait(barrier, peers)
@@ -207,13 +221,17 @@
 
         @pl.when(has_after)
         def _():
-            for s in range(slices):
-                send_objects(p, s).wait_recv()
+            send_objects(p, 0).wait_recv()
 
         @pl.when(has_after & (p > 0))
         def _():
             for s in reversed(range(slices)):
                 send_piece(p - 1, s).start()
+
+        @pl.when(has_after)
+        def _():
+            for s in range(1, slices):
+                send_objects(p, s).wait_recv()
 
         def window(s):
             own = [gathered(y, s, c) for c in range(2)]
@@ -304,14 +322,16 @@
     amount, width, _ = measured.shape
     factors = jnp.asarray(tables(width))
     windows = (amount, slices, 2, width, width)
-    small = pl.BlockSpec(memory_space=pltpu.SMEM)
     large = pl.BlockSpec(memory_space=pltpu.HBM)
     return pl.pallas_call(
         kernel,
         out_shape=pltpu.VMEM(objects.shape, jnp.float32),
-        in_specs=[small] * 3 + [large] * 4,
+        in_specs=[large] * 7,
         out_specs=pl.BlockSpec(memory_space=pltpu.VMEM),
         scratch_shapes=[
+            pltpu.SMEM(x_offsets.shape, jnp.int32),
+            pltpu.SMEM(y_offsets.shape, jnp.int32),
+            pltpu.SMEM(modes.shape, jnp.int32),
             pltpu.VMEM(objects.shape, jnp.float32),
             pltpu.VMEM(probes.shape, jnp.float32),
             pltpu.VMEM(measured.shape, jnp.float32),
@@ -324,6 +344,7 @@
             pltpu.VMEM(windows, jnp.float32),
             pltpu.VMEM(windows, jnp.float32),
             pltpu.VMEM(windows, jnp.float32),
+            pltpu.SemaphoreType.DMA((3,)),
             pltpu.SemaphoreType.DMA((slices,)),
             pltpu.SemaphoreType.DMA((3,)),
             pltpu.SemaphoreType.DMA((2,)),

time: 57.5 us -> 72.3 us (1.26)
  the two profiles are of different devices: /device:TPU:8 before, /device:TPU:14 now
where the time goes in v6:
time: 72.3 us; the launch traced here: 72.2 us
  Pallas kernels  70.2 us (97%)
  local copies, waits for them, and re-layouts  2.02 us (3%)
    pallas_call x1, Pallas kernels, on_device(): pl.pallas_call(kernel, out_shape=pltpu.VMEM(objects.shape, jnp.float32),...  70.2 us
    unnamed x1, local copies, waits for them, and re-layouts  2.02 us

profile of v6, /device:TPU:14, one launch (start us, length us, event | category | flops | bytes accessed | tf_op | source)
XLA Modules:
  0.0 72.2 jit_solution(3893175598775757071)
XLA Ops:
  0.0 70.2 %gradient_step.1 = f32[2,2,256,1024]{3,2,1,0:T(8,128)S(1)} custom-call(s32[2]{0:T(128)} %x_hbm.1, s32[2]{0:T(128)} %y_hbm.1, s32[2]{0:T(128)} %mode_hbm.1, f32[2,2,256,1024]{3,2,1,0:T(8,128)} %objects_hbm.1, f32[2,2,256,256]{3,2,1,0:T(8,128)} %probes_hbm.1, f32[2,256,256]{2,1,0:T(8,128)} %measured_hbm.1, f32[2,2,256,256]{3,2,1,0:T(8,128)} %constant.2.clone.tables_hbm), custom_call_target="tpu_custom_call" | custom-call | flops 6442450944 | bytes 16777216 | tf_op jit(solution)/shard_map/gradient_step/pallas_call | solution.py:326
  70.2 2.0 %copy.9 = f32[2,2,256,1024]{3,2,1,0:T(8,128)} copy(f32[2,2,256,1024]{3,2,1,0:T(8,128)S(1)} %gradient_step.1) | data formatting | bytes 8388608

commit v7 on v6

--- a/solution.py
+++ b/solution.py
@@ -175,8 +175,7 @@
                 y = place_before[amount + p]
                 for c in range(2):
                     packed[p, s, c] = gathered(y, s, c)
-                if p == 0:
-                    send_objects(p, s).start()
+                send_objects(p, s).start()
 
     for copy in others:
         copy.start()
@@ -208,12 +207,6 @@
                     left[i, first, further] = part
 
     def visit(p, carry):
-        @pl.when(has_before & (p + 1 < amount))
-        def _():
-            for s in range(slices):
-                send_objects(p, s).wait_send()
-                send_objects(p + 1, s).start()
-
         x, y, mode = x_ref[p], y_ref[p], mode_ref[p]
         inside = row >= x
         shift = lax.rem(y, width)
@@ -221,18 +214,14 @@
 
         @pl.when(has_after)
         def _():
-            send_objects(p, 0).wait_recv()
+            for s in range(slices):
+                send_objects(p, s).wait_recv()
 
         @pl.when(has_after & (p > 0))
         def _():
             for s in reversed(range(slices)):
                 send_piece(p - 1, s).start()
 
-        @pl.when(has_after)
-        def _():
-            for s in range(1, slices):
-                send_objects(p, s).wait_recv()
-
         def window(s):
             own = [gathered(y, s, c) for c in range(2)]
             return [jnp.where(inside, own[c], beyond[p, s, c]) for c in range(2)]
@@ -241,11 +230,9 @@
             pieces[p, s, 0] = piece[0]
             pieces[p, s, 1] = -piece[1]
 
-            if s > 0 or amount == 1:
-
-                @pl.when(has_after & (p == amount - 1))
-                def _():
-                    send_piece(p, s).start()
+            @pl.when(has_after & (p == amount - 1))
+            def _():
+                send_piece(p, s).start()
 
         move, far = (right[0], left[0]), (right[1], left[1])
         middle = transform(*times(entry, window(0)), *move)
@@ -271,14 +258,6 @@
         return carry
 
     lax.fori_loop(0, slices, own_update, 0)
-
-    if amount > 1:
-
-        @pl.when(has_after)
-        def _():
-            for s in reversed(range(slices)):
-                send_piece(amount - 2, s).wait_send()
-            send_piece(amount - 1, 0).start()
 
     def late_update(step, carry):
         p, s = step // slices, slices - 1 - step % slices
@@ -299,18 +278,16 @@
 
     lax.fori_loop(0, amount * slices, late_update, 0)
 
-    for s in range(slices):
-
-        @pl.when(has_before)
-        def _():
-            send_objects(amount - 1, s).wait_send()
-
-        for p in range(amount):
-            if p != amount - 2:
-
-                @pl.when(has_after)
-                def _():
-                    send_piece(p, s).wait_send()
+    for p in range(amount):
+        for s in range(slices):
+
+            @pl.when(has_before)
+            def _():
+                send_objects(p, s).wait_send()
+
+            @pl.when(has_after)
+            def _():
+                send_piece(p, s).wait_send()
 
     @pl.when(has_after)
     def _():

time: 72.3 us -> 56.8 us (0.79)
  the two profiles are of different devices: /device:TPU:14 before, /device:TPU:8 now
where the time goes in v7:
time: 56.8 us; the launch traced here: 56.7 us
  Pallas kernels  54.6 us (96%)
  local copies, waits for them, and re-layouts  2.02 us (4%)
    pallas_call x1, Pallas kernels, on_device(): pl.pallas_call(kernel, out_shape=pltpu.VMEM(objects.shape, jnp.float32),...  54.6 us
    unnamed x1, local copies, waits for them, and re-layouts  2.02 us

profile of v7, /device:TPU:8, one launch (start us, length us, event | category | flops | bytes accessed | tf_op | source)
XLA Modules:
  0.0 56.7 jit_solution(289679601337671463)
XLA Ops:
  0.0 54.6 %gradient_step.1 = f32[2,2,256,1024]{3,2,1,0:T(8,128)S(1)} custom-call(s32[2]{0:T(128)} %x_hbm.1, s32[2]{0:T(128)} %y_hbm.1, s32[2]{0:T(128)} %mode_hbm.1, f32[2,2,256,1024]{3,2,1,0:T(8,128)} %objects_hbm.1, f32[2,2,256,256]{3,2,1,0:T(8,128)} %probes_hbm.1, f32[2,256,256]{2,1,0:T(8,128)} %measured_hbm.1, f32[2,2,256,256]{3,2,1,0:T(8,128)} %constant.2.clone.tables_hbm), custom_call_target="tpu_custom_call" | custom-call | flops 6442450944 | bytes 16777216 | tf_op jit(solution)/shard_map/gradient_step/pallas_call | solution.py:303
  54.6 2.0 %copy.9 = f32[2,2,256,1024]{3,2,1,0:T(8,128)} copy(f32[2,2,256,1024]{3,2,1,0:T(8,128)S(1)} %gradient_step.1) | data formatting | bytes 8388608

commit v8 on v7

--- a/solution.py
+++ b/solution.py
@@ -94,13 +94,13 @@
     def send_place():
         return send(place, place_before, (place_sem.at[0], place_sem.at[1]), after)
 
-    def send_objects(p, s):
-        sems = (object_sem.at[0, p, s], object_sem.at[1, p, s])
-        return send(packed.at[p, s], beyond.at[p, s], sems, before)
-
-    def send_piece(p, s):
-        sems = (piece_sem.at[0, p, s], piece_sem.at[1, p, s])
-        return send(pieces.at[p, s], returned.at[p, s], sems, after)
+    def send_objects(p, s, c):
+        sems = (object_sem.at[0, p, s, c], object_sem.at[1, p, s, c])
+        return send(packed.at[p, s, c], beyond.at[p, s, c], sems, before)
+
+    def send_piece(p, s, c):
+        sems = (piece_sem.at[0, p, s, c], piece_sem.at[1, p, s, c])
+        return send(pieces.at[p, s, c], returned.at[p, s, c], sems, after)
 
     load_objects = [
         pltpu.make_async_copy(objects_hbm.at[s], objects.at[s], object_load_sem.at[s])
@@ -175,7 +175,7 @@
                 y = place_before[amount + p]
                 for c in range(2):
                     packed[p, s, c] = gathered(y, s, c)
-                send_objects(p, s).start()
+                    send_objects(p, s, c).start()
 
     for copy in others:
         copy.start()
@@ -215,12 +215,14 @@
         @pl.when(has_after)
         def _():
             for s in range(slices):
-                send_objects(p, s).wait_recv()
+                for c in range(2):
+                    send_objects(p, s, c).wait_recv()
 
         @pl.when(has_after & (p > 0))
         def _():
             for s in reversed(range(slices)):
-                send_piece(p - 1, s).start()
+                for c in range(2):
+                    send_piece(p - 1, s, c).start()
 
         def window(s):
             own = [gathered(y, s, c) for c in range(2)]
@@ -232,7 +234,8 @@
 
             @pl.when(has_after & (p == amount - 1))
             def _():
-                send_piece(p, s).start()
+                for c in range(2):
+                    send_piece(p, s, c).start()
 
         move, far = (right[0], left[0]), (right[1], left[1])
         middle = transform(*times(entry, window(0)), *move)
@@ -264,10 +267,10 @@
 
         @pl.when(has_before)
         def _():
-            send_piece(p, s).wait_recv()
             x, y = place_before[p], place_before[amount + p]
             inside = row < x
             for c in range(2):
+                send_piece(p, s, c).wait_recv()
                 piece = jnp.where(inside, returned[p, s, c], 0.0)
                 for k in range(span // width):
                     kept = jnp.where(across(y, k), piece, 0.0)
@@ -283,11 +286,13 @@
 
             @pl.when(has_before)
             def _():
-                send_objects(p, s).wait_send()
+                for c in range(2):
+                    send_objects(p, s, c).wait_send()
 
             @pl.when(has_after)
             def _():
-                send_piece(p, s).wait_send()
+                for c in range(2):
+                    send_piece(p, s, c).wait_send()
 
     @pl.when(has_after)
     def _():
@@ -325,8 +330,8 @@
             pltpu.SemaphoreType.DMA((slices,)),
             pltpu.SemaphoreType.DMA((3,)),
             pltpu.SemaphoreType.DMA((2,)),
-            pltpu.SemaphoreType.DMA((2, amount, slices)),
-            pltpu.SemaphoreType.DMA((2, amount, slices)),
+            pltpu.SemaphoreType.DMA((2, amount, slices, 2)),
+            pltpu.SemaphoreType.DMA((2, amount, slices, 2)),
         ],
         compiler_params=pltpu.CompilerParams(
             collective_id=0, has_side_effects=True, vmem_limit_bytes=VMEM_BYTES

time: 56.8 us -> 56.8 us (level)
  no operation moved by 1% of the time
where the time goes in v8:
time: 56.8 us; the launch traced here: 56.6 us
  Pallas kernels  54.6 us (96%)
  local copies, waits for them, and re-layouts  2.02 us (4%)
    pallas_call x1, Pallas kernels, on_device(): pl.pallas_call(kernel, out_shape=pltpu.VMEM(objects.shape, jnp.float32),...  54.6 us
    unnamed x1, local copies, waits for them, and re-layouts  2.02 us

profile of v8, /device:TPU:8, one launch (start us, length us, event | category | flops | bytes accessed | tf_op | source)
XLA Modules:
  0.0 56.6 jit_solution(9432633276372260272)
XLA Ops:
  0.0 54.6 %gradient_step.1 = f32[2,2,256,1024]{3,2,1,0:T(8,128)S(1)} custom-call(s32[2]{0:T(128)} %x_hbm.1, s32[2]{0:T(128)} %y_hbm.1, s32[2]{0:T(128)} %mode_hbm.1, f32[2,2,256,1024]{3,2,1,0:T(8,128)} %objects_hbm.1, f32[2,2,256,256]{3,2,1,0:T(8,128)} %probes_hbm.1, f32[2,256,256]{2,1,0:T(8,128)} %measured_hbm.1, f32[2,2,256,256]{3,2,1,0:T(8,128)} %constant.2.clone.tables_hbm), custom_call_target="tpu_custom_call" | custom-call | flops 6442450944 | bytes 16777216 | tf_op jit(solution)/shard_map/gradient_step/pallas_call | solution.py:308
  54.6 2.0 %copy.9 = f32[2,2,256,1024]{3,2,1,0:T(8,128)} copy(f32[2,2,256,1024]{3,2,1,0:T(8,128)S(1)} %gradient_step.1) | data formatting | bytes 8388608
